TPU v7x, 32 devices: a whole 2x2x4 slice. The times are simulated.
32 devices in a mesh: groups: 2 (over y), ctx: 4 (over z), dp: 2 (over x), mp: 2 (over core).
Axes of the slice: x: 2, y: 2, z: 4, core: 2. Of those that a mesh axis runs over, the one named last changes fastest.
Arguments:
- teacher_rows: bfloat16 [2, 8192, 4096], P('dp', ('groups', 'ctx'), 'mp'), parts along dimension 1, may hold values from -6 to 6
- student_hidden: bfloat16 [2, 6144, 1536], P('dp', ('groups', 'ctx'), 'mp'), parts along dimension 1, may hold values from -6 to 6
- projector: bfloat16 [4096, 1536], P(None, 'mp'), may hold values from -0.09375 to 0.09375
- span_end: int32 [2, 6144], P('dp', ('groups', 'ctx')), parts along dimension 1, may hold values from 1 to 4096, as said below
Outputs:
- token_loss: float32 [2, 6144], P('dp', ('groups', 'ctx')), parts along dimension 1
- w_grad: float32 [8192, 1536], P(('groups', 'ctx', 'dp'), 'mp'), parts along dimension 0
There are 2 independent parts, one for each index of `groups`. A program takes and returns all parts, laid end to end along the dimension named above; an argument that names none is the same for every part. Nothing has to cross between parts.
Inputs may be any that keep to these rules, and one draw needn't show every extreme that they name: `span_end`: ends rise by 1 or more from token to token and the last of a document is 4096. The end of student token i * 768 - 1 lies within 128 of i * 1024 for every i, and in every document it is exactly i * 1024 + 128 or i * 1024 - 128 for some i. Student token i * 768 spans exactly one teacher token for every i.
All inputs are finite; a program needn't handle non-finite values.
Results may differ from a plain program's by a relative error of at most 0.0033.
Values may be sent and summed in bfloat16 or wider, within the bound.
A program may use at most 128 MiB of HBM per device.

v0:
```python
import jax
import jax.numpy as jnp
from jax import lax
from jax.sharding import PartitionSpec as P

epsilon = 1e-06


def shifted(block, axis, distance):
    devices = range(lax.axis_size(axis))
    route = [(i - distance, i) for i in devices if i - distance in devices]
    return lax.ppermute(block, axis, route)


def extended(value, sides, width):
    for axis, dim in sides:
        size, length = (lax.axis_size(axis), value.shape[dim])
        up = [(i, (i + 1) % size) for i in range(size - 1)]
        down = [(j, i) for i, j in up]
        last = lax.slice_in_dim(value, length - width, length, axis=dim)
        first = lax.slice_in_dim(value, 0, width, axis=dim)
        before = lax.ppermute(last, axis, up)
        after = lax.ppermute(first, axis, down)
        value = jnp.concatenate([before, value, after], axis=dim)
    return value


def body(teacher_rows, student_hidden, projector, span_end):
    teacher = teacher_rows[0]
    span_ends = span_end[0]
    teach_rows = teacher.shape[0]
    rim_width = teach_rows // 8
    earlier = shifted(span_ends[-1:], "ctx", 1)
    span_starts = jnp.concatenate([earlier, span_ends[:-1]])
    window = extended(teacher, (("ctx", 0),), rim_width)
    window_start = lax.axis_index("ctx") * teach_rows - rim_width
    positions = window_start + jnp.arange(teach_rows + 2 * rim_width, dtype=jnp.int32)
    member = (positions[None, :] >= span_starts[:, None]) & (
        positions[None, :] < span_ends[:, None]
    )
    sums = jnp.dot(member.astype(jnp.bfloat16), window, preferred_element_type=jnp.float32)
    counts = (span_ends - span_starts).astype(jnp.float32)
    pooled_half = (sums / counts[:, None]).astype(jnp.bfloat16)
    pooled = lax.all_gather(pooled_half, "mp", axis=1, tiled=True)
    projected = jnp.dot(pooled, projector, preferred_element_type=jnp.float32)
    hidden = student_hidden[0].astype(jnp.float32)
    inner, psq, hsq = lax.psum(
        (
            jnp.sum(projected * hidden, axis=1),
            jnp.sum(projected * projected, axis=1),
            jnp.sum(hidden * hidden, axis=1),
        ),
        "mp",
    )
    scale = lax.rsqrt((psq + epsilon) * (hsq + epsilon))
    token_loss = (1.0 - inner * scale)[None, :]
    proj_grad = (
        (inner * scale / (psq + epsilon))[:, None] * projected - scale[:, None] * hidden
    ).astype(jnp.bfloat16)
    w_grad = lax.psum_scatter(
        lax.dot_general(
            pooled, proj_grad, (((0,), (0,)), ((), ())), preferred_element_type=jnp.float32
        ),
        ("ctx", "dp"),
        scatter_dimension=0,
        tiled=True,
    )
    return (token_loss, w_grad)


def solution(mesh):
    return jax.shard_map(
        body,
        mesh=mesh,
        in_specs=(
            P("dp", ("groups", "ctx"), "mp"),
            P("dp", ("groups", "ctx"), "mp"),
            P(None, "mp"),
            P("dp", ("groups", "ctx")),
        ),
        out_specs=(P("dp", ("groups", "ctx")), P(("groups", "ctx", "dp"), "mp")),
        check_vma=False,
    )
```

profile of v0, /device:TPU:0, one launch (start us, length us, event | category | flops | bytes accessed | tf_op | source)
XLA Modules:
  0.0 294.1 jit_solution(15586300061459131241)
XLA Ops:
  7.2 0.0 all-gather.2.cloned.1.call-start
  7.2 1.3 slice_bitcast_fusion.1
  8.5 5.0 %collective-permute-start.1 = (bf16[128,2048]{1,0:T(8,128)(2,1)S(1)}, bf16[128,2048]{1,0:T(8,128)(2,1)S(1)}, u32[]{:S(2)}, u32[]{:S(2)}) collective-permute-start(bf16[128,2048]{1,0:T(8,128)(2,1)S(1)} %get-tuple-element.12), channel_id=1, source_target_pairs={{0,4},{4,8},{8,12},{1,5},{5,9},{9,13},{2,6},{6,10},{10,14},{3,7},{... | collective-permute-start | bytes 1572872 | tf_op jit(solution)/shard_map/ppermute | solution.py:22
  13.5 1.3 collective-permute-start.2
  14.8 1.2 slice.24
  16.0 5.1 %collective-permute-start = (s32[1]{0:T(128)}, s32[1]{0:T(128)}, u32[]{:S(2)}, u32[]{:S(2)}) collective-permute-start(s32[1]{0:T(128)} %bitcast), channel_id=1, source_target_pairs={{0,4},{4,8},{8,12},{1,5},{5,9},{9,13},{2,6},{6,10},{10,14},{3,7},{... | collective-permute-start | bytes 20 | tf_op jit(solution)/shard_map/ppermute | solution.py:12
  21.1 0.7 reduce.1
  21.8 0.7 slice_reduce_fusion
  22.5 2.1 collective-permute-done
  24.6 0.8 subtract_convert_fusion
  25.4 0.0 collective-permute-done.1
  25.4 3.3 %collective-permute-done.2 = bf16[128,2048]{1,0:T(8,128)(2,1)S(1)} collective-permute-done((bf16[128,2048]{1,0:T(8,128)(2,1)S(1)}, bf16[128,2048]{1,0:T(8,128)(2,1)S(1)}, u32[]{:S(2)}, u32[]{:S(2)}) %collective-permute-start.2) | collective-permute-done | bytes 524320 | tf_op jit(solution)/shard_map/ppermute | solution.py:23
  28.7 0.0 copy-start
  28.7 8.2 %divide_convert_fusion = bf16[768,2048]{1,0:T(8,128)(2,1)} fusion(f32[768]{0:T(1024)S(1)} %get-tuple-element.10, bf16[128,2048]{1,0:T(8,128)(2,1)S(1)} %collective-permute-done.2, bf16[1024,2048]{1,0:T(8,128)(2,1)} %bitcast.17, bf16[128,2048]{1,0:T(8,128)(2,1)S(1)} %collective-permute-done.1, s32[1280]{0:T(1024)S(1)} %iota_add_fusion, s32[768]{0:T(1024)S(1)} %reduce.1, ...), kind=kOutput, calls=%fused_computation | convolution fusion | flops 4048355328 | bytes 8402944 | tf_op jit(solution)/shard_map/dot_general | solution.py:41
  37.0 0.0 all-gather.2.cloned.1.call-update
  37.0 0.0 reduce-scatter.2.cloned.1.call-start
  37.0 0.0 copy-done
  37.0 0.6 copy.6
  37.7 16.4 %all-gather.2.cloned.1.call-done = bf16[768,4096]{1,0:T(8,128)(2,1)} async-done(((bf16[768,2048]{1,0:T(8,128)(2,1)}), bf16[768,4096]{1,0:T(8,128)(2,1)}) %all-gather.2.cloned.1.call-update) | async-done | bytes 6291472 | tf_op jit(solution)/shard_map/all_gather | solution.py:44
  54.1 10.3 %multiply_reduce_fusion = (f32[768]{0:T(1024)S(1)}, f32[768]{0:T(1024)S(1)}, f32[768]{0:T(1024)S(1)}, f32[768,768]{0,1:T(8,128)}) fusion(bf16[1,768,768]{1,2,0:T(8,128)(2,1)S(1)} %copy.6, bf16[768,4096]{1,0:T(8,128)(2,1)} %all-gather.2.cloned.1.call-done, bf16[4096,768]{1,0:T(8,128)(2,1)} %param.6), kind=kOutput, calls=%fused_computation.17 | convolution fusion | flops 4835963904 | bytes 16131072 | tf_op jit(solution)/shard_map/dot_general | solution.py:45
  64.4 3.3 %all-reduce = (f32[768]{0:T(1024)S(1)}, f32[768]{0:T(1024)S(1)}, f32[768]{0:T(1024)S(1)}) all-reduce(f32[768]{0:T(1024)S(1)} %get-tuple-element.3, f32[768]{0:T(1024)S(1)} %get-tuple-element.4, f32[768]{0:T(1024)S(1)} %get-tuple-element.2), channel_id=1, replica_groups=mesh['groups'=2,'ctx'=4,'dp'=2,'mp'=2] {'mp'}, use_global_device_ids=true, to_apply=%region_1.0 | all-reduce | flops 2304 | bytes 18432 | tf_op jit(solution)/shard_map/psum | solution.py:47
  67.7 10.8 %fusion.20 = f32[4096,768]{1,0:T(8,128)} fusion(bf16[768,4096]{1,0:T(8,128)(2,1)} %all-gather.2.cloned.1.call-done, f32[768,768]{0,1:T(8,128)} %get-tuple-element.14, bf16[1,768,768]{1,2,0:T(8,128)(2,1)S(1)} %copy.6, f32[768]{0:T(1024)S(1)} %get-tuple-element.9, f32[768]{0:T(1024)S(1)} %get-tuple-element.8), kind=kOutput, calls=%fused_computation.21 | convolution fusion | flops 4834787328 | bytes 22419456 | tf_op jit(solution)/shard_map/dot_general | solution.py:61
  78.6 0.0 reduce-scatter.2.cloned.1.call-update
  78.6 0.6 broadcast_in_dim.2
  79.2 208.1 %reduce-scatter.2.cloned.1.call-done = f32[512,768]{1,0:T(8,128)} async-done(((f32[4096,768]{1,0:T(8,128)}), f32[512,768]{1,0:T(8,128)}) %reduce-scatter.2.cloned.1.call-update) | async-done | bytes 1572880 | tf_op jit(solution)/shard_map/reduce_scatter | solution.py:60
  (3 shorter events, 0.0 us)
Async XLA Ops:
  7.2 46.9 %all-gather.2.cloned.1.call-start = ((), (), s32[]{:S(2)}) async-start(), calls=%async_computation.1 | async-start | bytes 9437184 | tf_op jit(solution)/shard_map/all_gather | solution.py:44
  8.5 16.9 %collective-permute-start.1 = (bf16[128,2048]{1,0:T(8,128)(2,1)S(1)}, bf16[128,2048]{1,0:T(8,128)(2,1)S(1)}, u32[]{:S(2)}, u32[]{:S(2)}) collective-permute-start(bf16[128,2048]{1,0:T(8,128)(2,1)S(1)} %get-tuple-element.12), channel_id=1, source_target_pairs={{0,4},{4,8},{8,12},{1,5},{5,9},{9,13},{2,6},{6,10},{10,14},{3,7},{... | collective-permute-start | bytes 1572872 | tf_op jit(solution)/shard_map/ppermute | solution.py:22
  13.5 15.3 %collective-permute-start.2 = (bf16[128,2048]{1,0:T(8,128)(2,1)S(1)}, bf16[128,2048]{1,0:T(8,128)(2,1)S(1)}, u32[]{:S(2)}, u32[]{:S(2)}) collective-permute-start(bf16[128,2048]{1,0:T(8,128)(2,1)S(1)} %get-tuple-element.13), channel_id=1, source_target_pairs={{4,0},{8,4},{12,8},{5,1},{9,5},{13,9},{6,2},{10,6},{14,10},{7,3},{... | collective-permute-start | bytes 1572872 | tf_op jit(solution)/shard_map/ppermute | solution.py:23
  16.0 8.6 %collective-permute-start = (s32[1]{0:T(128)}, s32[1]{0:T(128)}, u32[]{:S(2)}, u32[]{:S(2)}) collective-permute-start(s32[1]{0:T(128)} %bitcast), channel_id=1, source_target_pairs={{0,4},{4,8},{8,12},{1,5},{5,9},{9,13},{2,6},{6,10},{10,14},{3,7},{... | collective-permute-start | bytes 20 | tf_op jit(solution)/shard_map/ppermute | solution.py:12
  28.7 8.3 %copy-start = (bf16[1,768,768]{2,1,0:T(8,128)(2,1)S(1)}, bf16[1,768,768]{2,1,0:T(8,128)(2,1)}, u32[]{:S(2)}) copy-start(bf16[1,768,768]{2,1,0:T(8,128)(2,1)} %param.5) | copy-start | bytes 3538948
  37.0 250.3 %reduce-scatter.2.cloned.1.call-start = ((), (), s32[]{:S(2)}) async-start(), calls=%async_computation.2 | async-start | bytes 14155776 | tf_op jit(solution)/shard_map/reduce_scatter | solution.py:60
Sparse Core Ops, SparseCore 0:
  37.1 16.9 all-gather.1
  78.7 208.5 reduce-scatter.1
where the time goes:
time: 294 us
  waiting for transfers between devices  230 us (78%)
  matrix products  29.4 us (10%)
  between operations  14.1 us (5%)
  starting transfers between devices  11.5 us (4%)
  local copies, waits for them, and re-layouts  4.44 us (2%)
  blocking collectives  3.32 us (1%)
    reduce_scatter x1, waiting for transfers between devices, body(): lax.psum_scatter(lax.dot_general(pooled, proj_grad, (((0,), (0,)), ((), (...  208 us
    all_gather x1, waiting for transfers between devices, body(): pooled = lax.all_gather(pooled_half, 'mp', axis=1, tiled=True)  16.4 us
    dot_general x1, matrix products, body(): lax.dot_general(pooled, proj_grad, (((0,), (0,)), ((), ())), preferred_el...  10.8 us
    dot_general x1, matrix products, body(): projected = jnp.dot(pooled, projector, preferred_element_type=jnp.float32)  10.3 us
    dot_general x1, matrix products, body(): jnp.dot(member.astype(jnp.bfloat16), window, preferred_element_type=jnp.f...  8.22 us
  transfers between devices with their start and end apart: 5, of which 4 were waited for; matrix products, arithmetic and copies ran while one was open for 2% of the time, Pallas kernels for 0%

commit v1 on v0

--- a/solution.py
+++ b/solution.py
@@ -1,9 +1,338 @@
 import jax
 import jax.numpy as jnp
 from jax import lax
+from jax.experimental import pallas as pl
+from jax.experimental.pallas import tpu as pltpu
 from jax.sharding import PartitionSpec as P
 
 epsilon = 1e-06
+MESH = pl.DeviceIdType.MESH
+F32 = jnp.float32
+BF16 = jnp.bfloat16
+
+
+def remote(src, dst, send, recv, device):
+    return pltpu.make_async_remote_copy(
+        src_ref=src, dst_ref=dst, send_sem=send, recv_sem=recv,
+        device_id=device, device_id_type=MESH,
+    )
+
+
+def kernel(
+    teach, hid, weight, end_ref, loss_ref, out_ref,
+    window, wbuf, hbuf, pool, other, proj, pg, pgo, sbuf, rbuf,
+    start_col, end_col, stat, stat_in,
+    loc_sem, halo_s, halo_r, mp_s, mp_r, x_s, x_r, f_s, f_r,
+    st_s, st_r, pg_s, pg_r, z_s, z_r,
+):
+    rows, rim = teach.shape[0], teach.shape[0] // 8
+    tokens = hid.shape[0]
+    chunk = pool.shape[2]
+    blocks, width = pg.shape[0], pg.shape[2]
+    c, p, m = (lax.axis_index("ctx"), lax.axis_index("dp"), lax.axis_index("mp"))
+    mate, twin = {"mp": 1 - m}, {"dp": 1 - p}
+    mine, theirs = 4 * m, 4 * (1 - m)
+
+    load_t = pltpu.make_async_copy(teach, window.at[pl.ds(rim, rows)], loc_sem.at[0])
+    load_w = pltpu.make_async_copy(weight, wbuf, loc_sem.at[1])
+    load_h = pltpu.make_async_copy(hid, hbuf, loc_sem.at[2])
+    load_t.start()
+    load_w.start()
+    load_h.start()
+
+    barrier = pltpu.get_barrier_semaphore()
+    for step in (1, 2, 3):
+        pl.semaphore_signal(
+            barrier, inc=1, device_id={"ctx": lax.rem(c + step, 4)}, device_id_type=MESH
+        )
+    pl.semaphore_signal(barrier, inc=1, device_id=mate, device_id_type=MESH)
+    pl.semaphore_signal(barrier, inc=1, device_id=twin, device_id_type=MESH)
+    pl.semaphore_wait(barrier, 5)
+
+    before = window.at[pl.ds(0, rim)]
+    after = window.at[pl.ds(rim + rows, rim)]
+    halo_up = remote(
+        teach.at[pl.ds(rows - rim, rim)], before, halo_s.at[0], halo_r.at[0],
+        {"ctx": lax.rem(c + 1, 4)},
+    )
+    halo_down = remote(
+        teach.at[pl.ds(0, rim)], after, halo_s.at[1], halo_r.at[1],
+        {"ctx": lax.rem(c + 3, 4)},
+    )
+
+    @pl.when(c < 3)
+    def _():
+        halo_up.start()
+
+    @pl.when(c > 0)
+    def _():
+        halo_down.start()
+
+    @pl.when(c == 0)
+    def _():
+        before[...] = jnp.zeros((rim, window.shape[1]), BF16)
+
+    @pl.when(c == 3)
+    def _():
+        after[...] = jnp.zeros((rim, window.shape[1]), BF16)
+
+    ends = jnp.broadcast_to(end_ref[...], (8, tokens)) - (c * rows - rim)
+    lane = lax.broadcasted_iota(jnp.int32, (8, tokens), 1)
+    starts = jnp.where(lane == 0, ends - 1, pltpu.roll(ends, 1, 1))
+    for i in range(tokens // 128):
+        at = slice(i * 128, i * 128 + 128)
+        end_col[at, :] = jnp.broadcast_to(ends[0:1, at], (128, 128)).T
+        start_col[at, :] = jnp.broadcast_to(starts[0:1, at], (128, 128)).T
+
+    def pool_block(first, count, low, depth):
+        at = pl.ds(first, count)
+        begin, stop = start_col[at, 0:1], end_col[at, 0:1]
+        place = low + lax.broadcasted_iota(jnp.int32, (count, depth), 1)
+        member = jnp.where((place >= begin) & (place < stop), 1.0, 0.0).astype(BF16)
+        share = 1.0 / (stop - begin).astype(F32)
+        for q in range(4):
+            sums = jnp.dot(
+                member, window[pl.ds(low, depth), q * chunk:(q + 1) * chunk],
+                preferred_element_type=F32,
+            )
+            pool[mine + q, at, :] = (sums * share).astype(BF16)
+
+    pieces = ((rim, tokens - 2 * rim), (0, rim), (tokens - rim, rim))
+
+    def mp_copy(i, slots):
+        ref = pool.at[pl.ds(slots, 4), pl.ds(*pieces[i])]
+        return remote(ref, ref, mp_s.at[i], mp_r.at[i], mate)
+
+    def x_copy(i, k):
+        return remote(
+            pool.at[mine + 2 * k + 1 - p, pl.ds(*pieces[i])],
+            other.at[2 * m + k, pl.ds(*pieces[i])],
+            x_s.at[i, k], x_r.at[i, k], twin,
+        )
+
+    def f_copy(i, k, half):
+        ref = other.at[2 * half + k, pl.ds(*pieces[i])]
+        return remote(ref, ref, f_s.at[i, k], f_r.at[i, k], mate)
+
+    def share_piece(i):
+        mp_copy(i, mine).start()
+        x_copy(i, 0).start()
+        x_copy(i, 1).start()
+
+    def project(first, count, base, fresh):
+        at = pl.ds(first, count)
+        total = jnp.dot(pool[base, at, :], wbuf[base], preferred_element_type=F32)
+        for q in range(1, 4):
+            total += jnp.dot(
+                pool[base + q, at, :], wbuf[base + q], preferred_element_type=F32
+            )
+        proj[at, :] = total if fresh else proj[at, :] + total
+
+    middle = tokens - 2 * rim
+    half = middle // 2
+    reach = rows - tokens + 2 * rim
+    load_t.wait()
+    for i in range(2):
+        low = rim + i * half
+        pool_block(low, half, low, half + reach)
+    share_piece(0)
+    load_w.wait()
+    for i in range(2):
+        project(rim + i * half, half, mine, True)
+
+    @pl.when(c > 0)
+    def _():
+        halo_up.wait_recv()
+
+    pool_block(0, rim, 0, rim + reach)
+    share_piece(1)
+
+    @pl.when(c < 3)
+    def _():
+        halo_down.wait_recv()
+
+    pool_block(tokens - rim, rim, tokens - rim, rim + reach)
+    share_piece(2)
+    project(0, rim, mine, True)
+    project(tokens - rim, rim, mine, True)
+    mp_copy(0, theirs).wait_recv()
+    for i in range(2):
+        project(rim + i * half, half, theirs, False)
+    mp_copy(1, theirs).wait_recv()
+    project(0, rim, theirs, False)
+    mp_copy(2, theirs).wait_recv()
+    project(tokens - rim, rim, theirs, False)
+    load_h.wait()
+
+    place = lax.broadcasted_iota(jnp.int32, (128, 128), 1)
+    for i in range(tokens // 128):
+        at = slice(i * 128, i * 128 + 128)
+        projected, hidden = proj[at, :], hbuf[at, :].astype(F32)
+        inner = jnp.sum(projected * hidden, axis=1, keepdims=True)
+        psq = jnp.sum(projected * projected, axis=1, keepdims=True)
+        hsq = jnp.sum(hidden * hidden, axis=1, keepdims=True)
+        packed = jnp.where(place == 0, inner, jnp.where(place == 1, psq, hsq))
+        stat[:, at] = packed.T[0:8, :]
+    swap = remote(stat, stat_in, st_s, st_r, mate)
+    swap.start()
+    swap.wait()
+    total = stat[...] + stat_in[...]
+    inner, psq, hsq = total[0:1], total[1:2], total[2:3]
+    scale = lax.rsqrt((psq + epsilon) * (hsq + epsilon))
+    loss_ref[...] = 1.0 - inner * scale
+    ratio = inner * scale / (psq + epsilon)
+    for i in range(tokens // 128):
+        at = slice(i * 128, i * 128 + 128)
+        a = jnp.broadcast_to(ratio[:, at], (128, 128)).T[:, 0:1]
+        b = jnp.broadcast_to(scale[:, at], (128, 128)).T[:, 0:1]
+        grad = (a * proj[at, :] - b * hbuf[at, :].astype(F32)).astype(BF16)
+        for j in range(blocks):
+            pg[j, at, :] = grad[:, j * width:(j + 1) * width]
+
+    def pg_copy(j):
+        return remote(pg.at[j], pgo.at[j], pg_s.at[j], pg_r.at[j], twin)
+
+    for j in range(blocks):
+        pg_copy(j).start()
+    for i in range(3):
+        for k in range(2):
+            x_copy(i, k).wait_recv()
+            f_copy(i, k, m).start()
+    for i in range(3):
+        for k in range(2):
+            f_copy(i, k, 1 - m).wait_recv()
+
+    upper = c // 2
+    edge = c * (1 - upper) + (3 - c) * upper
+
+    def mirrored(d):
+        return d * (1 - upper) + (3 - d) * upper
+
+    def partial(d, j):
+        dims = (((0,), (0,)), ((), ()))
+        return lax.dot_general(
+            pool[2 * d + p], pg[j], dims, preferred_element_type=F32
+        ) + lax.dot_general(other[d], pgo[j], dims, preferred_element_type=F32)
+
+    routes = (
+        (mirrored(3 - edge), mirrored(1 + edge), edge),
+        (mirrored(2 - 2 * edge), mirrored(2 - 2 * edge), 2),
+        (mirrored(1 + 2 * edge), mirrored(1 + 2 * edge), 3),
+    )
+
+    def z_copy(s, j):
+        _, device, slot = routes[s]
+        return remote(
+            sbuf.at[s, j], rbuf.at[slot, j], z_s.at[s, j], z_r.at[slot, j],
+            {"ctx": device},
+        )
+
+    def landed(slot, j):
+        ref = rbuf.at[slot, j]
+        remote(
+            ref, ref, z_s.at[0, j], z_r.at[slot, j], {"ctx": lax.rem(c + 1, 4)}
+        ).wait_recv()
+
+    def send_block(j, carry):
+        pg_copy(j).wait_recv()
+        for s in range(2):
+            sbuf[s, j] = partial(routes[s][0], j).astype(BF16)
+            z_copy(s, j).start()
+        value = partial(routes[2][0], j)
+
+        @pl.when(edge == 0)
+        def _():
+            sbuf[2, j] = value.astype(BF16)
+
+        @pl.when(edge == 1)
+        def _():
+            landed(0, j)
+            sbuf[2, j] = (value + rbuf[0, j].astype(F32)).astype(BF16)
+
+        z_copy(2, j).start()
+        return carry
+
+    lax.fori_loop(0, blocks, send_block, 0)
+    for j in range(blocks):
+        out_ref[:, j * width:(j + 1) * width] = partial(c, j)
+    for j in range(blocks):
+        at = slice(j * width, (j + 1) * width)
+
+        @pl.when(edge == 1)
+        def _():
+            landed(1, j)
+            out_ref[:, at] += rbuf[1, j].astype(F32)
+
+        landed(2, j)
+        landed(3, j)
+        out_ref[:, at] += rbuf[2, j].astype(F32) + rbuf[3, j].astype(F32)
+
+    @pl.when(c < 3)
+    def _():
+        halo_up.wait_send()
+
+    @pl.when(c > 0)
+    def _():
+        halo_down.wait_send()
+
+    for i in range(3):
+        mp_copy(i, mine).wait_send()
+        for k in range(2):
+            x_copy(i, k).wait_send()
+            f_copy(i, k, m).wait_send()
+    for j in range(blocks):
+        pg_copy(j).wait_send()
+        for s in range(3):
+            z_copy(s, j).wait_send()
+
+
+def fused(teacher_rows, student_hidden, projector, span_end):
+    rows, features = teacher_rows.shape[1:]
+    tokens, columns = student_hidden.shape[1:]
+    depth = 2 * features
+    chunk, blocks = depth // 8, 3
+    width, rim = columns // blocks, rows // 8
+    anywhere = pl.BlockSpec(memory_space=pl.ANY)
+    local = pl.BlockSpec(memory_space=pltpu.VMEM)
+    dma = pltpu.SemaphoreType.DMA
+    return tuple(pl.pallas_call(
+        kernel,
+        out_shape=(
+            jax.ShapeDtypeStruct((1, tokens), F32),
+            jax.ShapeDtypeStruct((chunk, columns), F32),
+        ),
+        in_specs=[anywhere, anywhere, anywhere, local],
+        out_specs=(local, local),
+        scratch_shapes=[
+            pltpu.VMEM((rows + 2 * rim, features), BF16),
+            pltpu.VMEM((8, chunk, columns), BF16),
+            pltpu.VMEM((tokens, columns), BF16),
+            pltpu.VMEM((8, tokens, chunk), BF16),
+            pltpu.VMEM((4, tokens, chunk), BF16),
+            pltpu.VMEM((tokens, columns), F32),
+            pltpu.VMEM((blocks, tokens, width), BF16),
+            pltpu.VMEM((blocks, tokens, width), BF16),
+            pltpu.VMEM((3, blocks, chunk, width), BF16),
+            pltpu.VMEM((4, blocks, chunk, width), BF16),
+            pltpu.VMEM((tokens, 128), jnp.int32),
+            pltpu.VMEM((tokens, 128), jnp.int32),
+            pltpu.VMEM((8, tokens), F32),
+            pltpu.VMEM((8, tokens), F32),
+            dma((3,)), dma((2,)), dma((2,)), dma((3,)), dma((3,)),
+            dma((3, 2)), dma((3, 2)), dma((3, 2)), dma((3, 2)),
+            dma, dma, dma((blocks,)), dma((blocks,)),
+            dma((3, blocks)), dma((4, blocks)),
+        ],
+        compiler_params=pltpu.CompilerParams(
+            collective_id=0, has_side_effects=True, vmem_limit_bytes=56 * 1024 * 1024
+        ),
+        cost_estimate=pl.CostEstimate(
+            flops=14_000_000_000, bytes_accessed=14_000_000, transcendentals=768
+        ),
+    )(
+        teacher_rows[0], student_hidden[0],
+        projector.reshape(8, chunk, columns), span_end,
+    ))
 
 
 def shifted(block, axis, distance):
@@ -69,8 +398,9 @@
 
 
 def solution(mesh):
+    sizes = tuple(mesh.shape[axis] for axis in ("ctx", "dp", "mp"))
     return jax.shard_map(
-        body,
+        fused if sizes == (4, 2, 2) else body,
         mesh=mesh,
         in_specs=(
             P("dp", ("groups", "ctx"), "mp"),

time: 294 us -> 112 us (0.38)
  waiting for transfers between devices: 230 us -> 0 us
  Pallas kernels: 0 us -> 107 us
  matrix products: 29.4 us -> 0 us
  between operations: 14.1 us -> 0.64 us
  starting transfers between devices: 11.5 us -> 0 us
  blocking collectives: 3.32 us -> 0 us
    reduce_scatter x1 -> x0, waiting for transfers between devices: 208 us -> none  [body(): lax.psum_scatter(lax.dot_general(pooled, proj_grad, (((0,), (0,)), ((), (...]
    pallas_call x0 -> x1, Pallas kernels: none -> 107 us  [fused(): pl.pallas_call(kernel, out_shape=(jax.ShapeDtypeStruct((1, tokens), F32),...]
    dot_general x3 -> x0, matrix products: 29.4 us -> none  [the longest x1 10.8 us: body(): lax.dot_general(pooled, proj_grad, (((0,), (0,)), ((), ())), preferred_el...]
    all_gather x1 -> x0, waiting for transfers between devices: 16.4 us -> none  [body(): pooled = lax.all_gather(pooled_half, 'mp', axis=1, tiled=True)]
    ppermute x3 -> x0, starting transfers between devices: 11.4 us -> none  [the longest x1 5.13 us: shifted(): return lax.ppermute(block, axis, route)]
    ppermute x3 -> x0, waiting for transfers between devices: 5.43 us -> none  [the longest x1 3.33 us: extended(): after = lax.ppermute(first, axis, down)]
    psum x1 -> x0, blocking collectives: 3.32 us -> none  [body(): lax.psum((jnp.sum(projected * hidden, axis=1), jnp.sum(projected * projec...]
    unnamed x3 -> x2, local copies, waits for them, and re-layouts: 0.65 us -> 3.9 us
  transfers between devices with their start and end apart: 5 -> 0, of which waited for: 4 -> 0; matrix products, arithmetic and copies ran while one was open for 2% -> 0% of each run, Pallas kernels for 0% -> 0%
where the time goes in v1:
time: 112 us
  Pallas kernels  107 us (96%)
  local copies, waits for them, and re-layouts  3.9 us (3%)
    pallas_call x1, Pallas kernels, fused(): pl.pallas_call(kernel, out_shape=(jax.ShapeDtypeStruct((1, tokens), F32),...  107 us
    unnamed x2, local copies, waits for them, and re-layouts  3.9 us

profile of v1, /device:TPU:0, one launch (start us, length us, event | category | flops | bytes accessed | tf_op | source)
XLA Modules:
  0.0 112.0 jit_solution(14600205571386743638)
XLA Ops:
  0.6 107.4 %shard_map.59 = (f32[1,768]{1,0:T(1,128)}, f32[512,768]{1,0:T(8,128)}) custom-call(bf16[1024,2048]{1,0:T(8,128)(2,1)} %bitcast.4, bf16[768,768]{1,0:T(8,128)(2,1)} %bitcast.5, bf16[8,512,768]{2,1,0:T(8,128)(2,1)} %bitcast.3, s32[1,768]{1,0:T(1,128)} %end_ref.1), custom_call_target="tpu_custom_call" | custom-call | flops 14000000000 | bytes 14000000 | tf_op jit(solution)/shard_map/pallas_call | solution.py:298
  108.0 1.3 %copy.8 = f32[1,768]{1,0:T(1,128)} copy(f32[1,768]{1,0:T(1,128)} %get-tuple-element.4) | data formatting | bytes 6144
  109.3 2.7 %copy.9 = f32[512,768]{1,0:T(8,128)} copy(f32[512,768]{1,0:T(8,128)} %get-tuple-element.5) | data formatting | bytes 3145728

commit v2 on v1

--- a/solution.py
+++ b/solution.py
@@ -84,8 +84,8 @@
         end_col[at, :] = jnp.broadcast_to(ends[0:1, at], (128, 128)).T
         start_col[at, :] = jnp.broadcast_to(starts[0:1, at], (128, 128)).T
 
-    def pool_block(first, count, low, depth):
-        at = pl.ds(first, count)
+    def pool_block(top, count, low, depth):
+        at = pl.ds(top, count)
         begin, stop = start_col[at, 0:1], end_col[at, 0:1]
         place = low + lax.broadcasted_iota(jnp.int32, (count, depth), 1)
         member = jnp.where((place >= begin) & (place < stop), 1.0, 0.0).astype(BF16)
@@ -97,30 +97,53 @@
             )
             pool[mine + q, at, :] = (sums * share).astype(BF16)
 
+    first, second = 1 - lax.rem(c, 2), lax.rem(c, 2)
+    upper = c // 2
+    edge = c * (1 - upper) + (3 - c) * upper
+    near = m + upper == 1
     pieces = ((rim, tokens - 2 * rim), (0, rim), (tokens - rim, rim))
 
     def mp_copy(i, slots):
         ref = pool.at[pl.ds(slots, 4), pl.ds(*pieces[i])]
         return remote(ref, ref, mp_s.at[i], mp_r.at[i], mate)
 
-    def x_copy(i, k):
+    def x_copy(i, turn, k):
         return remote(
             pool.at[mine + 2 * k + 1 - p, pl.ds(*pieces[i])],
             other.at[2 * m + k, pl.ds(*pieces[i])],
-            x_s.at[i, k], x_r.at[i, k], twin,
+            x_s.at[i, turn], x_r.at[i, turn], twin,
         )
 
-    def f_copy(i, k, half):
-        ref = other.at[2 * half + k, pl.ds(*pieces[i])]
-        return remote(ref, ref, f_s.at[i, k], f_r.at[i, k], mate)
+    def f_copy(i, turn, k, owner):
+        ref = other.at[2 * owner + k, pl.ds(*pieces[i])]
+        return remote(ref, ref, f_s.at[i, turn], f_r.at[i, turn], mate)
+
+    def x_start(turn, k):
+        for i in range(3):
+            x_copy(i, turn, k).start()
+
+    def forward(turn, k):
+        for i in range(3):
+            x_copy(i, turn, k).wait_recv()
+            f_copy(i, turn, k, m).start()
+
+    def forwarded(turn, k):
+        for i in range(3):
+            f_copy(i, turn, k, 1 - m).wait_recv()
 
     def share_piece(i):
         mp_copy(i, mine).start()
-        x_copy(i, 0).start()
-        x_copy(i, 1).start()
-
-    def project(first, count, base, fresh):
-        at = pl.ds(first, count)
+
+        @pl.when((edge == 1) | near)
+        def _():
+            x_copy(i, 0, first).start()
+
+        @pl.when((edge == 0) & near)
+        def _():
+            x_copy(i, 1, second).start()
+
+    def project(top, count, base, fresh):
+        at = pl.ds(top, count)
         total = jnp.dot(pool[base, at, :], wbuf[base], preferred_element_type=F32)
         for q in range(1, 4):
             total += jnp.dot(
@@ -192,18 +215,22 @@
     def pg_copy(j):
         return remote(pg.at[j], pgo.at[j], pg_s.at[j], pg_r.at[j], twin)
 
-    for j in range(blocks):
-        pg_copy(j).start()
-    for i in range(3):
-        for k in range(2):
-            x_copy(i, k).wait_recv()
-            f_copy(i, k, m).start()
-    for i in range(3):
-        for k in range(2):
-            f_copy(i, k, 1 - m).wait_recv()
-
-    upper = c // 2
-    edge = c * (1 - upper) + (3 - c) * upper
+    pg_copy(0).start()
+
+    @pl.when(edge == 1)
+    def _():
+        forward(0, first)
+        forwarded(0, first)
+
+    @pl.when((edge == 0) & near)
+    def _():
+        forward(0, first)
+        forward(1, second)
+
+    @pl.when((edge == 0) & (m + upper != 1))
+    def _():
+        forwarded(0, first)
+        forwarded(1, second)
 
     def mirrored(d):
         return d * (1 - upper) + (3 - d) * upper
@@ -234,10 +261,18 @@
         ).wait_recv()
 
     def send_block(j, carry):
-        pg_copy(j).wait_recv()
+        pg_copy(j).wait()
+
+        @pl.when(j + 1 < blocks)
+        def _():
+            pg_copy(j + 1).start()
+
         for s in range(2):
             sbuf[s, j] = partial(routes[s][0], j).astype(BF16)
             z_copy(s, j).start()
+        return carry
+
+    def send_last(j, carry):
         value = partial(routes[2][0], j)
 
         @pl.when(edge == 0)
@@ -253,6 +288,39 @@
         return carry
 
     lax.fori_loop(0, blocks, send_block, 0)
+
+    far = m + upper != 1
+
+    @pl.when((edge == 1) & near)
+    def _():
+        x_start(1, second)
+        forward(1, second)
+
+    @pl.when((edge == 1) & far)
+    def _():
+        forwarded(1, second)
+        x_start(1, second)
+
+    @pl.when((edge == 0) & near)
+    def _():
+        forwarded(0, first)
+
+    @pl.when((edge == 0) & far)
+    def _():
+        x_start(0, first)
+        forward(0, first)
+        x_start(1, second)
+
+    lax.fori_loop(0, blocks, send_last, 0)
+
+    @pl.when(near)
+    def _():
+        forwarded(1, second)
+
+    @pl.when(far)
+    def _():
+        forward(1, second)
+
     for j in range(blocks):
         out_ref[:, j * width:(j + 1) * width] = partial(c, j)
     for j in range(blocks):
@@ -277,11 +345,10 @@
 
     for i in range(3):
         mp_copy(i, mine).wait_send()
-        for k in range(2):
-            x_copy(i, k).wait_send()
-            f_copy(i, k, m).wait_send()
+        for turn, k in ((0, first), (1, second)):
+            x_copy(i, turn, k).wait_send()
+            f_copy(i, turn, k, m).wait_send()
     for j in range(blocks):
-        pg_copy(j).wait_send()
         for s in range(3):
             z_copy(s, j).wait_send()
 

time: 112 us -> 98.6 us (0.88)
  Pallas kernels: 107 us -> 93.9 us
    pallas_call x1, Pallas kernels: 107 us -> 93.9 us  [fused(): pl.pallas_call(kernel, out_shape=(jax.ShapeDtypeStruct((1, tokens), F32),...]
where the time goes in v2:
time: 98.6 us; the launch traced here: 98.4 us
  Pallas kernels  93.9 us (95%)
  local copies, waits for them, and re-layouts  3.9 us (4%)
    pallas_call x1, Pallas kernels, fused(): pl.pallas_call(kernel, out_shape=(jax.ShapeDtypeStruct((1, tokens), F32),...  93.9 us
    unnamed x2, local copies, waits for them, and re-layouts  3.9 us

profile of v2, /device:TPU:0, one launch (start us, length us, event | category | flops | bytes accessed | tf_op | source)
XLA Modules:
  0.0 98.4 jit_solution(10143364018906972532)
XLA Ops:
  0.6 93.9 %shard_map.59 = (f32[1,768]{1,0:T(1,128)}, f32[512,768]{1,0:T(8,128)}) custom-call(bf16[1024,2048]{1,0:T(8,128)(2,1)} %bitcast.4, bf16[768,768]{1,0:T(8,128)(2,1)} %bitcast.5, bf16[8,512,768]{2,1,0:T(8,128)(2,1)} %bitcast.3, s32[1,768]{1,0:T(1,128)} %end_ref.1), custom_call_target="tpu_custom_call" | custom-call | flops 14000000000 | bytes 14000000 | tf_op jit(solution)/shard_map/pallas_call | solution.py:365
  94.5 1.3 %copy.8 = f32[1,768]{1,0:T(1,128)} copy(f32[1,768]{1,0:T(1,128)} %get-tuple-element.4) | data formatting | bytes 6144
  95.8 2.7 %copy.9 = f32[512,768]{1,0:T(8,128)} copy(f32[512,768]{1,0:T(8,128)} %get-tuple-element.5) | data formatting | bytes 3145728

commit v3 on v2

--- a/solution.py
+++ b/solution.py
@@ -162,6 +162,9 @@
     load_w.wait()
     for i in range(2):
         project(rim + i * half, half, mine, True)
+    mp_copy(0, theirs).wait_recv()
+    for i in range(2):
+        project(rim + i * half, half, theirs, False)
 
     @pl.when(c > 0)
     def _():
@@ -178,9 +181,6 @@
     share_piece(2)
     project(0, rim, mine, True)
     project(tokens - rim, rim, mine, True)
-    mp_copy(0, theirs).wait_recv()
-    for i in range(2):
-        project(rim + i * half, half, theirs, False)
     mp_copy(1, theirs).wait_recv()
     project(0, rim, theirs, False)
     mp_copy(2, theirs).wait_recv()

time: 98.6 us -> 96.8 us (0.982)
  Pallas kernels: 93.9 us -> 92 us
    pallas_call x1, Pallas kernels: 93.9 us -> 92 us  [fused(): pl.pallas_call(kernel, out_shape=(jax.ShapeDtypeStruct((1, tokens), F32),...]
where the time goes in v3:
time: 96.8 us; the launch traced here: 96.5 us
  Pallas kernels  92 us (95%)
  local copies, waits for them, and re-layouts  3.9 us (4%)
    pallas_call x1, Pallas kernels, fused(): pl.pallas_call(kernel, out_shape=(jax.ShapeDtypeStruct((1, tokens), F32),...  92 us
    unnamed x2, local copies, waits for them, and re-layouts  3.9 us

profile of v3, /device:TPU:0, one launch (start us, length us, event | category | flops | bytes accessed | tf_op | source)
XLA Modules:
  0.0 96.5 jit_solution(11799285110995225750)
XLA Ops:
  0.6 92.0 %shard_map.59 = (f32[1,768]{1,0:T(1,128)}, f32[512,768]{1,0:T(8,128)}) custom-call(bf16[1024,2048]{1,0:T(8,128)(2,1)} %bitcast.4, bf16[768,768]{1,0:T(8,128)(2,1)} %bitcast.5, bf16[8,512,768]{2,1,0:T(8,128)(2,1)} %bitcast.3, s32[1,768]{1,0:T(1,128)} %end_ref.1), custom_call_target="tpu_custom_call" | custom-call | flops 14000000000 | bytes 14000000 | tf_op jit(solution)/shard_map/pallas_call | solution.py:365
  92.6 1.3 %copy.8 = f32[1,768]{1,0:T(1,128)} copy(f32[1,768]{1,0:T(1,128)} %get-tuple-element.4) | data formatting | bytes 6144
  93.9 2.7 %copy.9 = f32[512,768]{1,0:T(8,128)} copy(f32[512,768]{1,0:T(8,128)} %get-tuple-element.5) | data formatting | bytes 3145728
